TPU v7x, 256 devices: a whole 4x4x8 slice. The times are simulated.
256 devices in a mesh: base: 32 (over x, y, core), band: 8 (over z).
Axes of the slice: x: 4, y: 4, z: 8, core: 2. Of those that a mesh axis runs over, the one named last changes fastest.
Arguments:
- visibilities: float32 [65536, 2, 128], P(('base', 'band')), may hold values from -6 to 6
- coords: float32 [65536, 2, 8], P(('base', 'band')), may hold values from -11.2 to 11.2
- chan_scale: float32 [16], replicated, may hold values from 0.9 to 1.1
- taper_gain: float32 [32, 32], replicated, may hold values from 0.25 to 1
- owner_base: int32 [65536, 1], P(('base', 'band')), may hold values from 0 to 31; in each aligned block of 256 rows (0 to 255, 256 to 511, ...) at most 16 rows name the same one
- tile_cell: int32 [65536], P(('base', 'band')), may hold values from 0 to 255
Outputs:
- image: float32 [2, 8192, 8192], P(None, ('base', 'band'))
Inputs may be any that keep to these rules, and one draw needn't show every extreme that they name: `owner_base`: among the 256 baselines of one device no value occurs more than 16 times, and in every draw some device has a value exactly 16 times.
All inputs are finite; a program needn't handle non-finite values.
Results may differ from a plain program's by a relative error of at most 0.0003.
Values sent between devices are 32-bit elements; how exact they have to be, the bound alone decides.
A program may use at most 128 MiB of HBM per device.

v0:
```python
import math
import jax
import jax.numpy as jnp
from jax import lax
from jax.sharding import PartitionSpec as P

G = 8192
two_pi = 2.0 * math.pi
exact = lax.Precision.HIGHEST


def phase_table(length, direction):
    indices = jnp.arange(length, dtype=jnp.int32)
    product = indices[:, None] * indices[None, :] % length
    angle = direction * two_pi / length * product.astype(jnp.float32)
    return (jnp.cos(angle), jnp.sin(angle))


def grid_block(samples, places, chan_scale, taper_gain):
    number = samples.shape[0]
    extent = taper_gain.shape[0]
    time_count = places.shape[2]
    sample_count = time_count * chan_scale.shape[0]
    offsets = (jnp.arange(extent, dtype=jnp.float32) - extent // 2) / extent
    u_pos = (places[:, 0, :, None] * chan_scale[None, None, :]).reshape(number, sample_count)
    v_pos = (places[:, 1, :, None] * chan_scale[None, None, :]).reshape(number, sample_count)
    angle_y = two_pi * offsets[None, :, None] * v_pos[:, None, :]
    angle_x = two_pi * offsets[None, :, None] * u_pos[:, None, :]
    cos_y = jnp.cos(angle_y)
    sin_y = jnp.sin(angle_y)
    cos_x = jnp.cos(angle_x)
    sin_x = jnp.sin(angle_x)
    real_in = samples[:, 0:1, :]
    imag_in = samples[:, 1:2, :]
    left_re = real_in * cos_y - imag_in * sin_y
    left_im = real_in * sin_y + imag_in * cos_y

    def pairwise(first_arr, second_arr):
        return jnp.einsum("nyv,nxv->nyx", first_arr, second_arr, precision=exact)

    pix_re = (pairwise(left_re, cos_x) - pairwise(left_im, sin_x)) * taper_gain
    pix_im = (pairwise(left_re, sin_x) + pairwise(left_im, cos_x)) * taper_gain
    f_cos, f_sin = phase_table(extent, 1.0)

    def along_x(values, table):
        return jnp.einsum("nyx,xk->nyk", values, table, precision=exact)

    def along_y(values, table):
        return jnp.einsum("yk,nyx->nkx", table, values, precision=exact)

    q_re = along_x(pix_re, f_cos) + along_x(pix_im, f_sin)
    q_im = along_x(pix_im, f_cos) - along_x(pix_re, f_sin)
    t_re = along_y(q_re, f_cos) + along_y(q_im, f_sin)
    t_im = along_y(q_im, f_cos) - along_y(q_re, f_sin)
    factor = 1.0 / (extent * math.sqrt(sample_count))
    return jnp.stack([t_re, t_im], axis=1).reshape(number, 2, extent * extent) * factor


def make_tiles(samples, places, chan_scale, taper_gain):
    number = samples.shape[0]
    block_size = math.gcd(number, 64)
    blocks = number // block_size

    def one_block(pieces):
        return grid_block(pieces[0], pieces[1], chan_scale, taper_gain)

    result = lax.map(
        one_block,
        (
            samples.reshape(blocks, block_size, 2, samples.shape[2]),
            places.reshape(blocks, block_size, 2, places.shape[2]),
        ),
    )
    return result.reshape(number, 2, result.shape[3])


def dft_last(real_part, imag_part):
    row_count = real_part.shape[0]
    length = real_part.shape[1]
    first_len = 2 ** ((length.bit_length() - 1) // 2)
    second_len = length // first_len
    cos_one, sin_one = phase_table(first_len, 1.0)
    cos_two, sin_two = phase_table(second_len, 1.0)
    real_in = real_part.reshape(row_count, first_len, second_len)
    imag_in = imag_part.reshape(row_count, first_len, second_len)

    def mix_first(values, table):
        return jnp.einsum("pab,ak->pkb", values, table, precision=exact)

    y_re = mix_first(real_in, cos_one) - mix_first(imag_in, sin_one)
    y_im = mix_first(real_in, sin_one) + mix_first(imag_in, cos_one)
    first_ids = jnp.arange(first_len, dtype=jnp.int32)
    second_ids = jnp.arange(second_len, dtype=jnp.int32)
    turns = first_ids[:, None] * second_ids[None, :] % length
    twist = two_pi / length * turns.astype(jnp.float32)
    twist_cos = jnp.cos(twist)
    twist_sin = jnp.sin(twist)
    z_re = y_re * twist_cos - y_im * twist_sin
    z_im = y_re * twist_sin + y_im * twist_cos

    def mix_second(values, table):
        return jnp.einsum("pkb,bm->pmk", values, table, precision=exact)

    out_re = mix_second(z_re, cos_two) - mix_second(z_im, sin_two)
    out_im = mix_second(z_re, sin_two) + mix_second(z_im, cos_two)
    return (out_re.reshape(row_count, length), out_im.reshape(row_count, length))


def shards(visibilities, coords, chan_scale, taper_gain, owner_base, tile_cell):
    n_base = lax.axis_size("base")
    n_band = lax.axis_size("band")
    slot_count = visibilities.shape[0]
    extent = taper_gain.shape[0]
    area = extent * extent
    capacity = 2 * slot_count // n_base
    buffer_len = capacity * n_base
    owners = owner_base[:, 0]
    onehot = (owners[:, None] == jnp.arange(n_base, dtype=jnp.int32)[None, :]).astype(jnp.int32)
    before = jnp.cumsum(onehot, axis=0) - onehot
    rank_in = jnp.sum(before * onehot, axis=1)
    target = rank_in * n_base + owners
    cell_slots = jnp.zeros((buffer_len,), jnp.float32).at[target].set(tile_cell.astype(jnp.float32))
    cell_slots = cell_slots.reshape(capacity, n_base)
    tiles = make_tiles(visibilities, coords, chan_scale, taper_gain)
    packed = jnp.zeros((buffer_len, 2, area), jnp.float32).at[target].set(tiles)
    packed = packed.reshape(capacity, n_base, 2, area)
    arrived, arrived_cells = (
        lax.all_to_all(packed, "base", split_axis=1, concat_axis=1, tiled=True),
        lax.all_to_all(cell_slots, "base", split_axis=1, concat_axis=1, tiled=True),
    )
    row_tiles = G // (extent * n_band)
    col_tiles = G // (extent * n_base)
    segment_ids = arrived_cells.reshape(buffer_len).astype(jnp.int32)
    summed = jax.ops.segment_sum(
        arrived.reshape(buffer_len, 2 * area), segment_ids, num_segments=row_tiles * col_tiles
    )
    uv_grid = summed.reshape(row_tiles, col_tiles, 2, extent, extent).transpose(2, 0, 3, 1, 4)
    uv_grid = uv_grid.reshape(2, row_tiles * extent, col_tiles * extent)
    row_major = lax.all_to_all(uv_grid, "base", split_axis=1, concat_axis=2, tiled=True)
    row_re, row_im = dft_last(row_major[0], row_major[1])
    returned = lax.all_to_all(
        jnp.stack([row_re, row_im]), "base", split_axis=2, concat_axis=1, tiled=True
    )
    flipped = jnp.transpose(returned, (0, 2, 1))
    col_major = lax.all_to_all(flipped, "band", split_axis=1, concat_axis=2, tiled=True)
    col_re, col_im = dft_last(col_major[0], col_major[1])
    return jnp.stack([col_re, col_im]) * (1.0 / G)


def solution(mesh):
    placed = (
        P(("base", "band"), None, None),
        P(("base", "band"), None, None),
        P(),
        P(),
        P(("base", "band"), None),
        P(("base", "band")),
    )
    return jax.shard_map(
        shards,
        mesh=mesh,
        in_specs=placed,
        out_specs=P(None, ("base", "band"), None),
        check_vma=False,
    )
```

profile of v0, /device:TPU:1, one launch (start us, length us, event | category | flops | bytes accessed | tf_op | source)
XLA Modules:
  0.0 582.1 jit_solution(8600578806524166067)
XLA Ops:
  5.8 8.6 %all-to-all-start = ((f32[16,32,1]{0,2,1:T(1,128)}), f32[16,32,1]{0,2,1:T(1,128)S(1)}, u32[]{:S(2)}, u32[]{:S(2)}) async-start(f32[16,32,1]{0,2,1:T(1,128)} %copy.184), calls=%async_computation | async-start | bytes 32768 | tf_op jit(solution)/shard_map/all_to_all | solution.py:129
  15.2 196.9 %while.12 = (s32[]{:T(128)}, f32[4,64,2,1024]{3,1,0,2:T(8,128)}, f32[4,64,2,128]{3,2,1,0:T(2,128)}, f32[4,64,2,8]{1,0,3,2:T(4,128)S(1)}, f32[16]{0:T(128)}, /*index=5*/f32[32,32]{1,0:T(8,128)}, s32[]{:T(128)}) while((s32[]{:T(128)}, f32[4,64,2,1024]{3,1,0,2:T(8,128)}, f32[4,64,2,128]{3,2,1,0:T(2,128)}, f32[4,64,2,8]{1,0,3,2:T(4,128)S(1)}, ...), condition=%wide.region_5.6_spmd, body=%wide.region_4.5_spmd.sunk | while | flops 610140224 | bytes 13221169 | solution.py:67
  17.4 8.9 %fusion.319 = f32[64,32,32]{2,1,0:T(8,128)S(1)} fusion(f32[64,128]{1,0:T(8,128)S(1)} %copy.248, f32[64,128]{1,0:T(8,128)S(1)} %get-tuple-element.192, f32[64,128]{1,0:T(8,128)S(1)} %copy.250, f32[32]{0:T(128)S(1)} %add_multiply_fusion.2, f32[64,128]{1,0:T(8,128)S(1)} %get-tuple-element.194), kind=kOutput, calls=%fused_computation.12.clone.1 | convolution fusion | flops 101974016 | bytes 393344 | tf_op jit(solution)/shard_map/while/body/eval_jaxpr/nyv,nxv->nyx/dot_general | solution.py:39
  26.3 9.4 %fusion.320 = f32[64,32,32]{2,1,0:T(8,128)S(1)} fusion(f32[64,32,32]{2,1,0:T(8,128)S(1)} %fusion.319, f32[32,32]{1,0:T(8,128)S(1)} %copy-done.2, f32[64,128]{1,0:T(8,128)S(1)} %copy.248, f32[64,128]{1,0:T(8,128)S(1)} %get-tuple-element.192, f32[64,128]{1,0:T(8,128)S(1)} %copy.250, f32[32]{0:T(128)S(1)} %add_multiply_fusion.2, ...), kind=kOutput, calls=%fused_computation.18.clone.1 | convolution fusion | flops 102105088 | bytes 659584 | tf_op jit(solution)/shard_map/while/body/eval_jaxpr/nyv,nxv->nyx/dot_general | solution.py:39
  37.0 9.0 %fusion.316 = f32[64,32,32]{2,1,0:T(8,128)S(1)} fusion(f32[64,128]{1,0:T(8,128)S(1)} %copy.248, f32[64,128]{1,0:T(8,128)S(1)} %get-tuple-element.192, f32[64,128]{1,0:T(8,128)S(1)} %copy.250, f32[32]{0:T(128)S(1)} %add_multiply_fusion.2, f32[64,128]{1,0:T(8,128)S(1)} %get-tuple-element.194), kind=kOutput, calls=%fused_computation.11.clone.1 | convolution fusion | flops 101974016 | bytes 393344 | tf_op jit(solution)/shard_map/while/body/eval_jaxpr/nyv,nxv->nyx/dot_general | solution.py:39
  46.0 9.1 %fusion.317 = f32[64,32,32]{2,1,0:T(8,128)S(1)} fusion(f32[64,32,32]{2,1,0:T(8,128)S(1)} %fusion.316, f32[32,32]{1,0:T(8,128)S(1)} %copy-done.2, f32[64,128]{1,0:T(8,128)S(1)} %copy.248, f32[64,128]{1,0:T(8,128)S(1)} %get-tuple-element.192, f32[64,128]{1,0:T(8,128)S(1)} %copy.250, f32[32]{0:T(128)S(1)} %add_multiply_fusion.2, ...), kind=kOutput, calls=%fused_computation.17.clone.1 | convolution fusion | flops 102105088 | bytes 659584 | tf_op jit(solution)/shard_map/while/body/eval_jaxpr/nyv,nxv->nyx/dot_general | solution.py:39
  65.8 8.9 %fusion.319 = f32[64,32,32]{2,1,0:T(8,128)S(1)} fusion(f32[64,128]{1,0:T(8,128)S(1)} %copy.248, f32[64,128]{1,0:T(8,128)S(1)} %get-tuple-element.192, f32[64,128]{1,0:T(8,128)S(1)} %copy.250, f32[32]{0:T(128)S(1)} %add_multiply_fusion.2, f32[64,128]{1,0:T(8,128)S(1)} %get-tuple-element.194), kind=kOutput, calls=%fused_computation.12.clone.1 | convolution fusion | flops 101974016 | bytes 393344 | tf_op jit(solution)/shard_map/while/body/eval_jaxpr/nyv,nxv->nyx/dot_general | solution.py:39
  74.6 9.1 %fusion.320 = f32[64,32,32]{2,1,0:T(8,128)S(1)} fusion(f32[64,32,32]{2,1,0:T(8,128)S(1)} %fusion.319, f32[32,32]{1,0:T(8,128)S(1)} %copy-done.2, f32[64,128]{1,0:T(8,128)S(1)} %copy.248, f32[64,128]{1,0:T(8,128)S(1)} %get-tuple-element.192, f32[64,128]{1,0:T(8,128)S(1)} %copy.250, f32[32]{0:T(128)S(1)} %add_multiply_fusion.2, ...), kind=kOutput, calls=%fused_computation.18.clone.1 | convolution fusion | flops 102105088 | bytes 659584 | tf_op jit(solution)/shard_map/while/body/eval_jaxpr/nyv,nxv->nyx/dot_general | solution.py:39
  84.9 9.1 %fusion.316 = f32[64,32,32]{2,1,0:T(8,128)S(1)} fusion(f32[64,128]{1,0:T(8,128)S(1)} %copy.248, f32[64,128]{1,0:T(8,128)S(1)} %get-tuple-element.192, f32[64,128]{1,0:T(8,128)S(1)} %copy.250, f32[32]{0:T(128)S(1)} %add_multiply_fusion.2, f32[64,128]{1,0:T(8,128)S(1)} %get-tuple-element.194), kind=kOutput, calls=%fused_computation.11.clone.1 | convolution fusion | flops 101974016 | bytes 393344 | tf_op jit(solution)/shard_map/while/body/eval_jaxpr/nyv,nxv->nyx/dot_general | solution.py:39
  94.0 9.3 %fusion.317 = f32[64,32,32]{2,1,0:T(8,128)S(1)} fusion(f32[64,32,32]{2,1,0:T(8,128)S(1)} %fusion.316, f32[32,32]{1,0:T(8,128)S(1)} %copy-done.2, f32[64,128]{1,0:T(8,128)S(1)} %copy.248, f32[64,128]{1,0:T(8,128)S(1)} %get-tuple-element.192, f32[64,128]{1,0:T(8,128)S(1)} %copy.250, f32[32]{0:T(128)S(1)} %add_multiply_fusion.2, ...), kind=kOutput, calls=%fused_computation.17.clone.1 | convolution fusion | flops 102105088 | bytes 659584 | tf_op jit(solution)/shard_map/while/body/eval_jaxpr/nyv,nxv->nyx/dot_general | solution.py:39
  113.7 8.9 %fusion.319 = f32[64,32,32]{2,1,0:T(8,128)S(1)} fusion(f32[64,128]{1,0:T(8,128)S(1)} %copy.248, f32[64,128]{1,0:T(8,128)S(1)} %get-tuple-element.192, f32[64,128]{1,0:T(8,128)S(1)} %copy.250, f32[32]{0:T(128)S(1)} %add_multiply_fusion.2, f32[64,128]{1,0:T(8,128)S(1)} %get-tuple-element.194), kind=kOutput, calls=%fused_computation.12.clone.1 | convolution fusion | flops 101974016 | bytes 393344 | tf_op jit(solution)/shard_map/while/body/eval_jaxpr/nyv,nxv->nyx/dot_general | solution.py:39
  122.6 9.1 %fusion.320 = f32[64,32,32]{2,1,0:T(8,128)S(1)} fusion(f32[64,32,32]{2,1,0:T(8,128)S(1)} %fusion.319, f32[32,32]{1,0:T(8,128)S(1)} %copy-done.2, f32[64,128]{1,0:T(8,128)S(1)} %copy.248, f32[64,128]{1,0:T(8,128)S(1)} %get-tuple-element.192, f32[64,128]{1,0:T(8,128)S(1)} %copy.250, f32[32]{0:T(128)S(1)} %add_multiply_fusion.2, ...), kind=kOutput, calls=%fused_computation.18.clone.1 | convolution fusion | flops 102105088 | bytes 659584 | tf_op jit(solution)/shard_map/while/body/eval_jaxpr/nyv,nxv->nyx/dot_general | solution.py:39
  133.0 9.3 %fusion.316 = f32[64,32,32]{2,1,0:T(8,128)S(1)} fusion(f32[64,128]{1,0:T(8,128)S(1)} %copy.248, f32[64,128]{1,0:T(8,128)S(1)} %get-tuple-element.192, f32[64,128]{1,0:T(8,128)S(1)} %copy.250, f32[32]{0:T(128)S(1)} %add_multiply_fusion.2, f32[64,128]{1,0:T(8,128)S(1)} %get-tuple-element.194), kind=kOutput, calls=%fused_computation.11.clone.1 | convolution fusion | flops 101974016 | bytes 393344 | tf_op jit(solution)/shard_map/while/body/eval_jaxpr/nyv,nxv->nyx/dot_general | solution.py:39
  142.2 9.1 %fusion.317 = f32[64,32,32]{2,1,0:T(8,128)S(1)} fusion(f32[64,32,32]{2,1,0:T(8,128)S(1)} %fusion.316, f32[32,32]{1,0:T(8,128)S(1)} %copy-done.2, f32[64,128]{1,0:T(8,128)S(1)} %copy.248, f32[64,128]{1,0:T(8,128)S(1)} %get-tuple-element.192, f32[64,128]{1,0:T(8,128)S(1)} %copy.250, f32[32]{0:T(128)S(1)} %add_multiply_fusion.2, ...), kind=kOutput, calls=%fused_computation.17.clone.1 | convolution fusion | flops 102105088 | bytes 659584 | tf_op jit(solution)/shard_map/while/body/eval_jaxpr/nyv,nxv->nyx/dot_general | solution.py:39
  161.8 8.9 %fusion.319 = f32[64,32,32]{2,1,0:T(8,128)S(1)} fusion(f32[64,128]{1,0:T(8,128)S(1)} %copy.248, f32[64,128]{1,0:T(8,128)S(1)} %get-tuple-element.192, f32[64,128]{1,0:T(8,128)S(1)} %copy.250, f32[32]{0:T(128)S(1)} %add_multiply_fusion.2, f32[64,128]{1,0:T(8,128)S(1)} %get-tuple-element.194), kind=kOutput, calls=%fused_computation.12.clone.1 | convolution fusion | flops 101974016 | bytes 393344 | tf_op jit(solution)/shard_map/while/body/eval_jaxpr/nyv,nxv->nyx/dot_general | solution.py:39
  170.6 9.3 %fusion.320 = f32[64,32,32]{2,1,0:T(8,128)S(1)} fusion(f32[64,32,32]{2,1,0:T(8,128)S(1)} %fusion.319, f32[32,32]{1,0:T(8,128)S(1)} %copy-done.2, f32[64,128]{1,0:T(8,128)S(1)} %copy.248, f32[64,128]{1,0:T(8,128)S(1)} %get-tuple-element.192, f32[64,128]{1,0:T(8,128)S(1)} %copy.250, f32[32]{0:T(128)S(1)} %add_multiply_fusion.2, ...), kind=kOutput, calls=%fused_computation.18.clone.1 | convolution fusion | flops 102105088 | bytes 659584 | tf_op jit(solution)/shard_map/while/body/eval_jaxpr/nyv,nxv->nyx/dot_general | solution.py:39
  181.2 9.0 %fusion.316 = f32[64,32,32]{2,1,0:T(8,128)S(1)} fusion(f32[64,128]{1,0:T(8,128)S(1)} %copy.248, f32[64,128]{1,0:T(8,128)S(1)} %get-tuple-element.192, f32[64,128]{1,0:T(8,128)S(1)} %copy.250, f32[32]{0:T(128)S(1)} %add_multiply_fusion.2, f32[64,128]{1,0:T(8,128)S(1)} %get-tuple-element.194), kind=kOutput, calls=%fused_computation.11.clone.1 | convolution fusion | flops 101974016 | bytes 393344 | tf_op jit(solution)/shard_map/while/body/eval_jaxpr/nyv,nxv->nyx/dot_general | solution.py:39
  190.2 9.1 %fusion.317 = f32[64,32,32]{2,1,0:T(8,128)S(1)} fusion(f32[64,32,32]{2,1,0:T(8,128)S(1)} %fusion.316, f32[32,32]{1,0:T(8,128)S(1)} %copy-done.2, f32[64,128]{1,0:T(8,128)S(1)} %copy.248, f32[64,128]{1,0:T(8,128)S(1)} %get-tuple-element.192, f32[64,128]{1,0:T(8,128)S(1)} %copy.250, f32[32]{0:T(128)S(1)} %add_multiply_fusion.2, ...), kind=kOutput, calls=%fused_computation.17.clone.1 | convolution fusion | flops 102105088 | bytes 659584 | tf_op jit(solution)/shard_map/while/body/eval_jaxpr/nyv,nxv->nyx/dot_general | solution.py:39
  218.4 26.5 %scatter_fusion = f32[512,2,1024]{2,1,0:T(2,128)} fusion(f32[512,2,1024]{2,1,0:T(2,128)} %broadcast_in_dim.11, s32[256]{0:T(256)S(1)} %bitcast.240, f32[256,2,1024]{2,1,0:T(2,128)S(1)} %copy.190), kind=kCustom, calls=%fused_computation.1 | custom fusion | bytes 6292480 | tf_op jit(solution)/shard_map/scatter | solution.py:125
  251.6 7.8 %all-to-all-start.1 = ((f32[16,32,2,1024]{3,2,0,1:T(2,128)}), f32[16,32,2,1024]{3,2,0,1:T(2,128)}, u32[]{:S(2)}, u32[]{:S(2)}) async-start(f32[16,32,2,1024]{3,2,0,1:T(2,128)} %copy.191), calls=%async_computation.1 | async-start | bytes 8388608 | tf_op jit(solution)/shard_map/all_to_all | solution.py:128
  259.6 51.9 %all-to-all-done.1 = f32[16,32,2,1024]{3,2,0,1:T(2,128)} async-done(((f32[16,32,2,1024]{3,2,0,1:T(2,128)}), f32[16,32,2,1024]{3,2,0,1:T(2,128)}, u32[]{:S(2)}, u32[]{:S(2)}) %all-to-all-start.1) | async-done | bytes 4194336 | tf_op jit(solution)/shard_map/all_to_all | solution.py:128
  319.7 8.9 %scatter_custom_fusion.2 = f32[256,2048]{1,0:T(8,128)S(1)} fusion(s32[512]{0:T(512)S(1)} %reshape.227, f32[512,2048]{1,0:T(8,128)} %bitcast.232, f32[]{:T(128)} %constant.129.clone.1), kind=kCustom, calls=%fused_computation.148 | custom fusion | flops 1048576 | bytes 2097664 | tf_op jit(solution)/shard_map/scatter-add | solution.py:134
  333.8 14.3 %copy.211 = f32[2,32,32,8,32]{4,3,0,2,1:T(8,128)} copy(f32[2,32,32,8,32]{4,2,0,3,1:T(8,128)} %bitcast.225) | data formatting | bytes 4194304 | tf_op jit(solution)/shard_map/reshape | solution.py:138
  348.1 7.7 %reshape.240 = f32[2,1024,256]{2,0,1:T(2,128)} reshape(f32[2,32,32,8,32]{4,3,0,2,1:T(8,128)} %copy.211) | data formatting | bytes 4194304 | tf_op jit(solution)/shard_map/reshape | solution.py:138
  355.8 7.4 %all-to-all-start.2 = ((f32[2,1024,256]{2,0,1:T(2,128)}), f32[2,1024,256]{2,0,1:T(2,128)S(1)}, u32[]{:S(2)}, u32[]{:S(2)}) async-start(f32[2,1024,256]{2,0,1:T(2,128)} %reshape.240), calls=%async_computation.2 | async-start | bytes 4194304 | tf_op jit(solution)/shard_map/all_to_all | solution.py:139
  363.4 28.0 %all-to-all-done.2 = f32[2,1024,256]{2,0,1:T(2,128)S(1)} async-done(((f32[2,1024,256]{2,0,1:T(2,128)}), f32[2,1024,256]{2,0,1:T(2,128)S(1)}, u32[]{:S(2)}, u32[]{:S(2)}) %all-to-all-start.2) | async-done | bytes 2097184 | tf_op jit(solution)/shard_map/all_to_all | solution.py:139
  416.1 7.9 %copy.200 = f32[2,32,8192]{1,0,2:T(2,128)} copy(f32[2,32,8192]{2,1,0:T(8,128)S(1)} %pad_maximum_fusion) | data formatting | bytes 4194304 | tf_op jit(solution)/shard_map/stack | solution.py:142
  423.9 10.2 %reshape.246 = f32[32,1,16384]{2,1,0:T(1,128)S(1)} reshape(f32[8192,2,32]{2,1,0:T(2,128)} %bitcast.223) | data formatting | bytes 4194304
  434.1 32.4 %all_to_all.62 = f32[32,1,16384]{2,1,0:T(1,128)} all-to-all(f32[32,1,16384]{2,1,0:T(1,128)S(1)} %reshape.246), channel_id=1, replica_groups=mesh['base'=32,'band'=8] {'base'}, dimensions={0} | all-to-all | bytes 4194304 | tf_op jit(solution)/shard_map/all_to_all | solution.py:141
  474.4 8.4 %reshape.247 = f32[8192,2,32]{2,1,0:T(2,128)} reshape(f32[32,16384]{1,0:T(8,128)S(1)} %reduce.2) | data formatting | bytes 4194304
  482.9 9.7 %copy.213 = f32[2,32,32,256]{3,1,2,0:T(8,128)S(1)} copy(f32[2,32,32,256]{1,0,3,2:T(2,128)} %bitcast.224) | data formatting | bytes 4194304 | tf_op jit(solution)/shard_map/all_to_all | solution.py:141
  495.0 60.2 %all_to_all.63 = f32[2,256,1024]{2,0,1:T(2,128)S(1)} all-to-all(f32[2,256,1024]{2,0,1:T(2,128)} %copy.203), channel_id=1, replica_groups=mesh['base'=32,'band'=8] {'band'}, dimensions={1} | all-to-all | bytes 4194304 | tf_op jit(solution)/shard_map/all_to_all | solution.py:145
  (182 shorter events, 140.0 us)
Async XLA Ops:
  5.8 245.8 %all-to-all-start = ((f32[16,32,1]{0,2,1:T(1,128)}), f32[16,32,1]{0,2,1:T(1,128)S(1)}, u32[]{:S(2)}, u32[]{:S(2)}) async-start(f32[16,32,1]{0,2,1:T(1,128)} %copy.184), calls=%async_computation | async-start | bytes 32768 | tf_op jit(solution)/shard_map/all_to_all | solution.py:129
  15.5 10.8 %copy-start.2 = (f32[32,32]{1,0:T(8,128)S(1)}, f32[32,32]{1,0:T(8,128)}, u32[]{:S(2)}) copy-start(f32[32,32]{1,0:T(8,128)} %get-tuple-element.214) | copy-start | bytes 12292 | tf_op jit(solution)/shard_map/while
  63.8 10.8 %copy-start.2 = (f32[32,32]{1,0:T(8,128)S(1)}, f32[32,32]{1,0:T(8,128)}, u32[]{:S(2)}) copy-start(f32[32,32]{1,0:T(8,128)} %get-tuple-element.214) | copy-start | bytes 12292 | tf_op jit(solution)/shard_map/while
  111.8 10.8 %copy-start.2 = (f32[32,32]{1,0:T(8,128)S(1)}, f32[32,32]{1,0:T(8,128)}, u32[]{:S(2)}) copy-start(f32[32,32]{1,0:T(8,128)} %get-tuple-element.214) | copy-start | bytes 12292 | tf_op jit(solution)/shard_map/while
  159.8 10.8 %copy-start.2 = (f32[32,32]{1,0:T(8,128)S(1)}, f32[32,32]{1,0:T(8,128)}, u32[]{:S(2)}) copy-start(f32[32,32]{1,0:T(8,128)} %get-tuple-element.214) | copy-start | bytes 12292 | tf_op jit(solution)/shard_map/while
  251.6 59.9 %all-to-all-start.1 = ((f32[16,32,2,1024]{3,2,0,1:T(2,128)}), f32[16,32,2,1024]{3,2,0,1:T(2,128)}, u32[]{:S(2)}, u32[]{:S(2)}) async-start(f32[16,32,2,1024]{3,2,0,1:T(2,128)} %copy.191), calls=%async_computation.1 | async-start | bytes 8388608 | tf_op jit(solution)/shard_map/all_to_all | solution.py:128
  355.8 35.6 %all-to-all-start.2 = ((f32[2,1024,256]{2,0,1:T(2,128)}), f32[2,1024,256]{2,0,1:T(2,128)S(1)}, u32[]{:S(2)}, u32[]{:S(2)}) async-start(f32[2,1024,256]{2,0,1:T(2,128)} %reshape.240), calls=%async_computation.2 | async-start | bytes 4194304 | tf_op jit(solution)/shard_map/all_to_all | solution.py:139
  396.4 1.2 copy-start
  561.0 1.2 copy-start.1
where the time goes:
time: 587 us; the launch traced here: 582 us
  matrix products  198 us (34%)
  local copies, waits for them, and re-layouts  156 us (27%)
  blocking collectives  92.7 us (16%)
  waiting for transfers between devices  79.9 us (14%)
  other arithmetic  24.8 us (4%)
  starting transfers between devices  23.8 us (4%)
  loops' own time  6.23 us (1%)
    dot_general x16, matrix products, pairwise(): return jnp.einsum('nyv,nxv->nyx', first_arr, second_arr, precision=exact)  145 us
    all_to_all x1, blocking collectives, shards(): lax.all_to_all(flipped, 'band', split_axis=1, concat_axis=2, tiled=True)  60.2 us
    all_to_all x1, waiting for transfers between devices, shards(): lax.all_to_all(packed, 'base', split_axis=1, concat_axis=1, tiled=True)  51.9 us
    all_to_all x1, blocking collectives, shards(): lax.all_to_all(jnp.stack([row_re, row_im]), 'base', split_axis=2, concat_...  32.4 us
    all_to_all x1, waiting for transfers between devices, shards(): lax.all_to_all(uv_grid, 'base', split_axis=1, concat_axis=2, tiled=True)  28 us
    scatter x1, local copies, waits for them, and re-layouts, shards(): packed = jnp.zeros((buffer_len, 2, area), jnp.float32).at[target].set(tiles)  26.5 us
    unnamed x7, local copies, waits for them, and re-layouts  22.6 us
    reshape x2, local copies, waits for them, and re-layouts, shards(): uv_grid = uv_grid.reshape(2, row_tiles * extent, col_tiles * extent)  22 us
  transfers between devices with their start and end apart: 3, of which 2 were waited for; matrix products, arithmetic and copies ran while one was open for 40% of the time, Pallas kernels for 0%

commit v1 on v0

--- a/solution.py
+++ b/solution.py
@@ -7,6 +7,12 @@
 G = 8192
 two_pi = 2.0 * math.pi
 exact = lax.Precision.HIGHEST
+
+
+def exchange_blocks(block, axis, split, join):
+    parts = jnp.split(block, lax.axis_size(axis), axis=split)
+    incoming = lax.all_to_all(jnp.stack(parts), axis, 0, 0)
+    return jnp.concatenate(incoming, axis=join)
 
 
 def phase_table(length, direction):
@@ -138,9 +144,7 @@
     uv_grid = uv_grid.reshape(2, row_tiles * extent, col_tiles * extent)
     row_major = lax.all_to_all(uv_grid, "base", split_axis=1, concat_axis=2, tiled=True)
     row_re, row_im = dft_last(row_major[0], row_major[1])
-    returned = lax.all_to_all(
-        jnp.stack([row_re, row_im]), "base", split_axis=2, concat_axis=1, tiled=True
-    )
+    returned = exchange_blocks(jnp.stack([row_re, row_im]), "base", 2, 1)
     flipped = jnp.transpose(returned, (0, 2, 1))
     col_major = lax.all_to_all(flipped, "band", split_axis=1, concat_axis=2, tiled=True)
     col_re, col_im = dft_last(col_major[0], col_major[1])

time: 587 us -> 542 us (0.923)
  local copies, waits for them, and re-layouts: 156 us -> 121 us
  other arithmetic: 24.8 us -> 16.1 us
    unnamed x7 -> x37, local copies, waits for them, and re-layouts: 22.6 us -> 5.5 us
    all_to_all x2 -> x0, local copies, waits for them, and re-layouts: 10.2 us -> none  [shards(): lax.all_to_all(jnp.stack([row_re, row_im]), 'base', split_axis=2, concat_...]
    another operation x4 -> x5, local copies, waits for them, and re-layouts: 11.8 us -> 4 us  [the longest x3 3.99 us: shards(): returned = exchange_blocks(jnp.stack([row_re, row_im]), 'base', 2, 1)]
    all_to_all x1 -> x0, other arithmetic: 7.39 us -> none  [shards(): lax.all_to_all(jnp.stack([row_re, row_im]), 'base', split_axis=2, concat_...]
  transfers between devices with their start and end apart: 3 -> 3, of which waited for: 2 -> 2; matrix products, arithmetic and copies ran while one was open for 40% -> 43% of each run, Pallas kernels for 0% -> 0%
where the time goes in v1:
time: 542 us; the launch traced here: 537 us
  matrix products  198 us (37%)
  local copies, waits for them, and re-layouts  121 us (22%)
  blocking collectives  91.6 us (17%)
  waiting for transfers between devices  79.9 us (15%)
  starting transfers between devices  24.1 us (4%)
  other arithmetic  16.1 us (3%)
  loops' own time  6.13 us (1%)
    dot_general x16, matrix products, pairwise(): return jnp.einsum('nyv,nxv->nyx', first_arr, second_arr, precision=exact)  145 us
    all_to_all x1, blocking collectives, shards(): lax.all_to_all(flipped, 'band', split_axis=1, concat_axis=2, tiled=True)  59.8 us
    all_to_all x1, waiting for transfers between devices, shards(): lax.all_to_all(packed, 'base', split_axis=1, concat_axis=1, tiled=True)  51.9 us
    all_to_all x1, blocking collectives, exchange_blocks(): incoming = lax.all_to_all(jnp.stack(parts), axis, 0, 0)  31.8 us
    all_to_all x1, waiting for transfers between devices, shards(): lax.all_to_all(uv_grid, 'base', split_axis=1, concat_axis=2, tiled=True)  28 us
    scatter x1, local copies, waits for them, and re-layouts, shards(): packed = jnp.zeros((buffer_len, 2, area), jnp.float32).at[target].set(tiles)  26.5 us
    reshape x2, local copies, waits for them, and re-layouts, shards(): uv_grid = uv_grid.reshape(2, row_tiles * extent, col_tiles * extent)  22 us
    dot_general x8, matrix products, mix_second(): return jnp.einsum('pkb,bm->pmk', values, table, precision=exact)  16.2 us
  transfers between devices with their start and end apart: 3, of which 2 were waited for; matrix products, arithmetic and copies ran while one was open for 43% of the time, Pallas kernels for 0%

profile of v1, /device:TPU:1, one launch (start us, length us, event | category | flops | bytes accessed | tf_op | source)
XLA Modules:
  0.0 537.4 jit_solution(10104104851454583800)
XLA Ops:
  5.8 8.6 %all-to-all-start = ((f32[16,32,1]{0,2,1:T(1,128)}), f32[16,32,1]{0,2,1:T(1,128)S(1)}, u32[]{:S(2)}, u32[]{:S(2)}) async-start(f32[16,32,1]{0,2,1:T(1,128)} %copy.182), calls=%async_computation | async-start | bytes 32768 | tf_op jit(solution)/shard_map/all_to_all | solution.py:135
  15.2 196.7 %while.12 = (s32[]{:T(128)}, f32[4,64,2,1024]{3,1,0,2:T(8,128)}, f32[4,64,2,128]{3,2,1,0:T(2,128)}, f32[4,64,2,8]{1,0,3,2:T(4,128)S(1)}, f32[16]{0:T(128)}, /*index=5*/f32[32,32]{1,0:T(8,128)}, s32[]{:T(128)}) while((s32[]{:T(128)}, f32[4,64,2,1024]{3,1,0,2:T(8,128)}, f32[4,64,2,128]{3,2,1,0:T(2,128)}, f32[4,64,2,8]{1,0,3,2:T(4,128)S(1)}, ...), condition=%wide.region_5.6_spmd, body=%wide.region_4.5_spmd.sunk | while | flops 610140224 | bytes 13221169 | solution.py:73
  17.3 8.9 %fusion.319 = f32[64,32,32]{2,1,0:T(8,128)S(1)} fusion(f32[64,128]{1,0:T(8,128)S(1)} %copy.242, f32[64,128]{1,0:T(8,128)S(1)} %get-tuple-element.192, f32[64,128]{1,0:T(8,128)S(1)} %copy.244, f32[32]{0:T(128)S(1)} %add_multiply_fusion.2, f32[64,128]{1,0:T(8,128)S(1)} %get-tuple-element.194), kind=kOutput, calls=%fused_computation.12.clone.1 | convolution fusion | flops 101974016 | bytes 393344 | tf_op jit(solution)/shard_map/while/body/eval_jaxpr/nyv,nxv->nyx/dot_general | solution.py:45
  26.2 9.1 %fusion.320 = f32[64,32,32]{2,1,0:T(8,128)S(1)} fusion(f32[64,32,32]{2,1,0:T(8,128)S(1)} %fusion.319, f32[32,32]{1,0:T(8,128)S(1)} %copy-done.2, f32[64,128]{1,0:T(8,128)S(1)} %copy.242, f32[64,128]{1,0:T(8,128)S(1)} %get-tuple-element.192, f32[64,128]{1,0:T(8,128)S(1)} %copy.244, f32[32]{0:T(128)S(1)} %add_multiply_fusion.2, ...), kind=kOutput, calls=%fused_computation.18.clone.1 | convolution fusion | flops 102105088 | bytes 659584 | tf_op jit(solution)/shard_map/while/body/eval_jaxpr/nyv,nxv->nyx/dot_general | solution.py:45
  36.5 9.3 %fusion.316 = f32[64,32,32]{2,1,0:T(8,128)S(1)} fusion(f32[64,128]{1,0:T(8,128)S(1)} %copy.242, f32[64,128]{1,0:T(8,128)S(1)} %get-tuple-element.192, f32[64,128]{1,0:T(8,128)S(1)} %copy.244, f32[32]{0:T(128)S(1)} %add_multiply_fusion.2, f32[64,128]{1,0:T(8,128)S(1)} %get-tuple-element.194), kind=kOutput, calls=%fused_computation.11.clone.1 | convolution fusion | flops 101974016 | bytes 393344 | tf_op jit(solution)/shard_map/while/body/eval_jaxpr/nyv,nxv->nyx/dot_general | solution.py:45
  45.8 9.1 %fusion.317 = f32[64,32,32]{2,1,0:T(8,128)S(1)} fusion(f32[64,32,32]{2,1,0:T(8,128)S(1)} %fusion.316, f32[32,32]{1,0:T(8,128)S(1)} %copy-done.2, f32[64,128]{1,0:T(8,128)S(1)} %copy.242, f32[64,128]{1,0:T(8,128)S(1)} %get-tuple-element.192, f32[64,128]{1,0:T(8,128)S(1)} %copy.244, f32[32]{0:T(128)S(1)} %add_multiply_fusion.2, ...), kind=kOutput, calls=%fused_computation.17.clone.1 | convolution fusion | flops 102105088 | bytes 659584 | tf_op jit(solution)/shard_map/while/body/eval_jaxpr/nyv,nxv->nyx/dot_general | solution.py:45
  65.3 8.9 %fusion.319 = f32[64,32,32]{2,1,0:T(8,128)S(1)} fusion(f32[64,128]{1,0:T(8,128)S(1)} %copy.242, f32[64,128]{1,0:T(8,128)S(1)} %get-tuple-element.192, f32[64,128]{1,0:T(8,128)S(1)} %copy.244, f32[32]{0:T(128)S(1)} %add_multiply_fusion.2, f32[64,128]{1,0:T(8,128)S(1)} %get-tuple-element.194), kind=kOutput, calls=%fused_computation.12.clone.1 | convolution fusion | flops 101974016 | bytes 393344 | tf_op jit(solution)/shard_map/while/body/eval_jaxpr/nyv,nxv->nyx/dot_general | solution.py:45
  74.2 9.3 %fusion.320 = f32[64,32,32]{2,1,0:T(8,128)S(1)} fusion(f32[64,32,32]{2,1,0:T(8,128)S(1)} %fusion.319, f32[32,32]{1,0:T(8,128)S(1)} %copy-done.2, f32[64,128]{1,0:T(8,128)S(1)} %copy.242, f32[64,128]{1,0:T(8,128)S(1)} %get-tuple-element.192, f32[64,128]{1,0:T(8,128)S(1)} %copy.244, f32[32]{0:T(128)S(1)} %add_multiply_fusion.2, ...), kind=kOutput, calls=%fused_computation.18.clone.1 | convolution fusion | flops 102105088 | bytes 659584 | tf_op jit(solution)/shard_map/while/body/eval_jaxpr/nyv,nxv->nyx/dot_general | solution.py:45
  84.7 9.0 %fusion.316 = f32[64,32,32]{2,1,0:T(8,128)S(1)} fusion(f32[64,128]{1,0:T(8,128)S(1)} %copy.242, f32[64,128]{1,0:T(8,128)S(1)} %get-tuple-element.192, f32[64,128]{1,0:T(8,128)S(1)} %copy.244, f32[32]{0:T(128)S(1)} %add_multiply_fusion.2, f32[64,128]{1,0:T(8,128)S(1)} %get-tuple-element.194), kind=kOutput, calls=%fused_computation.11.clone.1 | convolution fusion | flops 101974016 | bytes 393344 | tf_op jit(solution)/shard_map/while/body/eval_jaxpr/nyv,nxv->nyx/dot_general | solution.py:45
  93.8 9.1 %fusion.317 = f32[64,32,32]{2,1,0:T(8,128)S(1)} fusion(f32[64,32,32]{2,1,0:T(8,128)S(1)} %fusion.316, f32[32,32]{1,0:T(8,128)S(1)} %copy-done.2, f32[64,128]{1,0:T(8,128)S(1)} %copy.242, f32[64,128]{1,0:T(8,128)S(1)} %get-tuple-element.192, f32[64,128]{1,0:T(8,128)S(1)} %copy.244, f32[32]{0:T(128)S(1)} %add_multiply_fusion.2, ...), kind=kOutput, calls=%fused_computation.17.clone.1 | convolution fusion | flops 102105088 | bytes 659584 | tf_op jit(solution)/shard_map/while/body/eval_jaxpr/nyv,nxv->nyx/dot_general | solution.py:45
  113.5 8.9 %fusion.319 = f32[64,32,32]{2,1,0:T(8,128)S(1)} fusion(f32[64,128]{1,0:T(8,128)S(1)} %copy.242, f32[64,128]{1,0:T(8,128)S(1)} %get-tuple-element.192, f32[64,128]{1,0:T(8,128)S(1)} %copy.244, f32[32]{0:T(128)S(1)} %add_multiply_fusion.2, f32[64,128]{1,0:T(8,128)S(1)} %get-tuple-element.194), kind=kOutput, calls=%fused_computation.12.clone.1 | convolution fusion | flops 101974016 | bytes 393344 | tf_op jit(solution)/shard_map/while/body/eval_jaxpr/nyv,nxv->nyx/dot_general | solution.py:45
  122.4 9.1 %fusion.320 = f32[64,32,32]{2,1,0:T(8,128)S(1)} fusion(f32[64,32,32]{2,1,0:T(8,128)S(1)} %fusion.319, f32[32,32]{1,0:T(8,128)S(1)} %copy-done.2, f32[64,128]{1,0:T(8,128)S(1)} %copy.242, f32[64,128]{1,0:T(8,128)S(1)} %get-tuple-element.192, f32[64,128]{1,0:T(8,128)S(1)} %copy.244, f32[32]{0:T(128)S(1)} %add_multiply_fusion.2, ...), kind=kOutput, calls=%fused_computation.18.clone.1 | convolution fusion | flops 102105088 | bytes 659584 | tf_op jit(solution)/shard_map/while/body/eval_jaxpr/nyv,nxv->nyx/dot_general | solution.py:45
  132.7 9.1 %fusion.316 = f32[64,32,32]{2,1,0:T(8,128)S(1)} fusion(f32[64,128]{1,0:T(8,128)S(1)} %copy.242, f32[64,128]{1,0:T(8,128)S(1)} %get-tuple-element.192, f32[64,128]{1,0:T(8,128)S(1)} %copy.244, f32[32]{0:T(128)S(1)} %add_multiply_fusion.2, f32[64,128]{1,0:T(8,128)S(1)} %get-tuple-element.194), kind=kOutput, calls=%fused_computation.11.clone.1 | convolution fusion | flops 101974016 | bytes 393344 | tf_op jit(solution)/shard_map/while/body/eval_jaxpr/nyv,nxv->nyx/dot_general | solution.py:45
  141.8 9.3 %fusion.317 = f32[64,32,32]{2,1,0:T(8,128)S(1)} fusion(f32[64,32,32]{2,1,0:T(8,128)S(1)} %fusion.316, f32[32,32]{1,0:T(8,128)S(1)} %copy-done.2, f32[64,128]{1,0:T(8,128)S(1)} %copy.242, f32[64,128]{1,0:T(8,128)S(1)} %get-tuple-element.192, f32[64,128]{1,0:T(8,128)S(1)} %copy.244, f32[32]{0:T(128)S(1)} %add_multiply_fusion.2, ...), kind=kOutput, calls=%fused_computation.17.clone.1 | convolution fusion | flops 102105088 | bytes 659584 | tf_op jit(solution)/shard_map/while/body/eval_jaxpr/nyv,nxv->nyx/dot_general | solution.py:45
  161.5 8.9 %fusion.319 = f32[64,32,32]{2,1,0:T(8,128)S(1)} fusion(f32[64,128]{1,0:T(8,128)S(1)} %copy.242, f32[64,128]{1,0:T(8,128)S(1)} %get-tuple-element.192, f32[64,128]{1,0:T(8,128)S(1)} %copy.244, f32[32]{0:T(128)S(1)} %add_multiply_fusion.2, f32[64,128]{1,0:T(8,128)S(1)} %get-tuple-element.194), kind=kOutput, calls=%fused_computation.12.clone.1 | convolution fusion | flops 101974016 | bytes 393344 | tf_op jit(solution)/shard_map/while/body/eval_jaxpr/nyv,nxv->nyx/dot_general | solution.py:45
  170.4 9.1 %fusion.320 = f32[64,32,32]{2,1,0:T(8,128)S(1)} fusion(f32[64,32,32]{2,1,0:T(8,128)S(1)} %fusion.319, f32[32,32]{1,0:T(8,128)S(1)} %copy-done.2, f32[64,128]{1,0:T(8,128)S(1)} %copy.242, f32[64,128]{1,0:T(8,128)S(1)} %get-tuple-element.192, f32[64,128]{1,0:T(8,128)S(1)} %copy.244, f32[32]{0:T(128)S(1)} %add_multiply_fusion.2, ...), kind=kOutput, calls=%fused_computation.18.clone.1 | convolution fusion | flops 102105088 | bytes 659584 | tf_op jit(solution)/shard_map/while/body/eval_jaxpr/nyv,nxv->nyx/dot_general | solution.py:45
  180.8 9.3 %fusion.316 = f32[64,32,32]{2,1,0:T(8,128)S(1)} fusion(f32[64,128]{1,0:T(8,128)S(1)} %copy.242, f32[64,128]{1,0:T(8,128)S(1)} %get-tuple-element.192, f32[64,128]{1,0:T(8,128)S(1)} %copy.244, f32[32]{0:T(128)S(1)} %add_multiply_fusion.2, f32[64,128]{1,0:T(8,128)S(1)} %get-tuple-element.194), kind=kOutput, calls=%fused_computation.11.clone.1 | convolution fusion | flops 101974016 | bytes 393344 | tf_op jit(solution)/shard_map/while/body/eval_jaxpr/nyv,nxv->nyx/dot_general | solution.py:45
  190.0 9.1 %fusion.317 = f32[64,32,32]{2,1,0:T(8,128)S(1)} fusion(f32[64,32,32]{2,1,0:T(8,128)S(1)} %fusion.316, f32[32,32]{1,0:T(8,128)S(1)} %copy-done.2, f32[64,128]{1,0:T(8,128)S(1)} %copy.242, f32[64,128]{1,0:T(8,128)S(1)} %get-tuple-element.192, f32[64,128]{1,0:T(8,128)S(1)} %copy.244, f32[32]{0:T(128)S(1)} %add_multiply_fusion.2, ...), kind=kOutput, calls=%fused_computation.17.clone.1 | convolution fusion | flops 102105088 | bytes 659584 | tf_op jit(solution)/shard_map/while/body/eval_jaxpr/nyv,nxv->nyx/dot_general | solution.py:45
  218.2 26.5 %scatter_fusion = f32[512,2,1024]{2,1,0:T(2,128)} fusion(f32[512,2,1024]{2,1,0:T(2,128)} %broadcast_in_dim.11, s32[256]{0:T(256)S(1)} %bitcast.362, f32[256,2,1024]{2,1,0:T(2,128)S(1)} %copy.188), kind=kCustom, calls=%fused_computation.1 | custom fusion | bytes 6292480 | tf_op jit(solution)/shard_map/scatter | solution.py:131
  244.7 6.6 %copy.189 = f32[16,32,2,1024]{3,2,0,1:T(2,128)} copy(f32[16,32,2,1024]{3,2,1,0:T(2,128)} %bitcast.347) | data formatting | bytes 8388608 | tf_op jit(solution)/shard_map/reshape | solution.py:132
  251.4 7.8 %all-to-all-start.1 = ((f32[16,32,2,1024]{3,2,0,1:T(2,128)}), f32[16,32,2,1024]{3,2,0,1:T(2,128)}, u32[]{:S(2)}, u32[]{:S(2)}) async-start(f32[16,32,2,1024]{3,2,0,1:T(2,128)} %copy.189), calls=%async_computation.1 | async-start | bytes 8388608 | tf_op jit(solution)/shard_map/all_to_all | solution.py:134
  259.3 51.9 %all-to-all-done.1 = f32[16,32,2,1024]{3,2,0,1:T(2,128)} async-done(((f32[16,32,2,1024]{3,2,0,1:T(2,128)}), f32[16,32,2,1024]{3,2,0,1:T(2,128)}, u32[]{:S(2)}, u32[]{:S(2)}) %all-to-all-start.1) | async-done | bytes 4194336 | tf_op jit(solution)/shard_map/all_to_all | solution.py:134
  311.2 4.3 copy.190
  315.5 3.9 copy.214
  319.4 8.9 %scatter_custom_fusion.2 = f32[256,2048]{1,0:T(8,128)S(1)} fusion(s32[512]{0:T(512)S(1)} %reshape.235, f32[512,2048]{1,0:T(8,128)} %bitcast.354, f32[]{:T(128)} %constant.129.clone.1), kind=kCustom, calls=%fused_computation.147 | custom fusion | flops 1048576 | bytes 2097664 | tf_op jit(solution)/shard_map/scatter-add | solution.py:140
  328.4 5.0 reshape.213
  333.4 14.3 %copy.207 = f32[2,32,32,8,32]{4,3,0,2,1:T(8,128)} copy(f32[2,32,32,8,32]{4,2,0,3,1:T(8,128)} %bitcast.346) | data formatting | bytes 4194304 | tf_op jit(solution)/shard_map/reshape | solution.py:144
  347.6 7.7 %reshape.248 = f32[2,1024,256]{2,0,1:T(2,128)} reshape(f32[2,32,32,8,32]{4,3,0,2,1:T(8,128)} %copy.207) | data formatting | bytes 4194304 | tf_op jit(solution)/shard_map/reshape | solution.py:144
  355.4 7.7 %all-to-all-start.2 = ((f32[2,1024,256]{2,0,1:T(2,128)}), f32[2,1024,256]{2,0,1:T(2,128)S(1)}, u32[]{:S(2)}, u32[]{:S(2)}) async-start(f32[2,1024,256]{2,0,1:T(2,128)} %reshape.248), calls=%async_computation.2 | async-start | bytes 4194304 | tf_op jit(solution)/shard_map/all_to_all | solution.py:145
  363.2 28.0 %all-to-all-done.2 = f32[2,1024,256]{2,0,1:T(2,128)S(1)} async-done(((f32[2,1024,256]{2,0,1:T(2,128)}), f32[2,1024,256]{2,0,1:T(2,128)S(1)}, u32[]{:S(2)}, u32[]{:S(2)}) %all-to-all-start.2) | async-done | bytes 2097184 | tf_op jit(solution)/shard_map/all_to_all | solution.py:145
  416.4 31.8 %all_to_all.49 = f32[32,2,32,256]{3,2,1,0:T(8,128)S(1)} all-to-all(f32[32,2,32,256]{3,2,1,0:T(8,128)S(1)} %constant_dynamic-update-slice_fusion.3), channel_id=1, replica_groups=mesh['base'=32,'band'=8] {'base'}, dimensions={0} | all-to-all | bytes 4194304 | tf_op jit(solution)/shard_map/all_to_all | solution.py:14
  450.6 59.8 %all_to_all.50 = f32[2,256,1024]{2,0,1:T(2,128)S(1)} all-to-all(f32[2,256,1024]{2,0,1:T(2,128)} %copy.199), channel_id=1, replica_groups=mesh['base'=32,'band'=8] {'band'}, dimensions={1} | all-to-all | bytes 4194304 | tf_op jit(solution)/shard_map/all_to_all | solution.py:149
  (210 shorter events, 112.4 us)
Async XLA Ops:
  5.8 245.6 %all-to-all-start = ((f32[16,32,1]{0,2,1:T(1,128)}), f32[16,32,1]{0,2,1:T(1,128)S(1)}, u32[]{:S(2)}, u32[]{:S(2)}) async-start(f32[16,32,1]{0,2,1:T(1,128)} %copy.182), calls=%async_computation | async-start | bytes 32768 | tf_op jit(solution)/shard_map/all_to_all | solution.py:135
  15.4 10.8 %copy-start.2 = (f32[32,32]{1,0:T(8,128)S(1)}, f32[32,32]{1,0:T(8,128)}, u32[]{:S(2)}) copy-start(f32[32,32]{1,0:T(8,128)} %get-tuple-element.214) | copy-start | bytes 12292 | tf_op jit(solution)/shard_map/while
  63.4 10.8 %copy-start.2 = (f32[32,32]{1,0:T(8,128)S(1)}, f32[32,32]{1,0:T(8,128)}, u32[]{:S(2)}) copy-start(f32[32,32]{1,0:T(8,128)} %get-tuple-element.214) | copy-start | bytes 12292 | tf_op jit(solution)/shard_map/while
  111.6 10.8 %copy-start.2 = (f32[32,32]{1,0:T(8,128)S(1)}, f32[32,32]{1,0:T(8,128)}, u32[]{:S(2)}) copy-start(f32[32,32]{1,0:T(8,128)} %get-tuple-element.214) | copy-start | bytes 12292 | tf_op jit(solution)/shard_map/while
  159.6 10.8 %copy-start.2 = (f32[32,32]{1,0:T(8,128)S(1)}, f32[32,32]{1,0:T(8,128)}, u32[]{:S(2)}) copy-start(f32[32,32]{1,0:T(8,128)} %get-tuple-element.214) | copy-start | bytes 12292 | tf_op jit(solution)/shard_map/while
  251.4 59.8 %all-to-all-start.1 = ((f32[16,32,2,1024]{3,2,0,1:T(2,128)}), f32[16,32,2,1024]{3,2,0,1:T(2,128)}, u32[]{:S(2)}, u32[]{:S(2)}) async-start(f32[16,32,2,1024]{3,2,0,1:T(2,128)} %copy.189), calls=%async_computation.1 | async-start | bytes 8388608 | tf_op jit(solution)/shard_map/all_to_all | solution.py:134
  355.4 35.9 %all-to-all-start.2 = ((f32[2,1024,256]{2,0,1:T(2,128)}), f32[2,1024,256]{2,0,1:T(2,128)S(1)}, u32[]{:S(2)}, u32[]{:S(2)}) async-start(f32[2,1024,256]{2,0,1:T(2,128)} %reshape.248), calls=%async_computation.2 | async-start | bytes 4194304 | tf_op jit(solution)/shard_map/all_to_all | solution.py:145
  396.3 1.2 copy-start
  516.2 1.2 copy-start.1
